TPU v7x, 32 devices: a whole 2x2x4 slice. The times are simulated.
32 devices in a mesh: groups: 2 (over y), rel: 4 (over z), bin: 2 (over x), rep: 2 (over core).
Axes of the slice: x: 2, y: 2, z: 4, core: 2. Of those that a mesh axis runs over, the one named last changes fastest.
Arguments:
- footprint: bfloat16 [192, 128, 128], P(('groups', 'rel', 'bin', 'rep')), parts along dimension 0, as said below
- block_tile: int32 [192], P(('groups', 'rel', 'bin', 'rep')), parts along dimension 0, may hold values from 0 to 31, as said below
- log_release: float32 [1024, 32], P(('groups', 'rel')), parts along dimension 0, may hold values from -4 to 4
- prior_mean: float32 [1024, 32], P(('groups', 'rel')), parts along dimension 0, may hold values from -4 to 4
- prior_weight: float32 [1024, 32], P(('groups', 'rel')), parts along dimension 0, may hold values from 0.5 to 2
- observed: float32 [256, 32, 128], P(('groups', 'rel', 'bin', 'rep')), parts along dimension 0, may hold values from -6 to 6
- noise_weight: float32 [256, 32, 128], P(('groups', 'rel', 'bin', 'rep')), parts along dimension 0, may hold values from 0.5 to 2
- pixel_mask: int32 [256, 128], P(('groups', 'rel', 'bin', 'rep')), parts along dimension 0, may hold values 0 or 1
Outputs:
- release_new: float32 [1024, 32], P(('groups', 'rel'), ('bin', 'rep')), parts along dimension 0
- residual: float32 [256, 32, 128], P(('groups', 'rel', 'bin', 'rep')), parts along dimension 0
There are 2 independent parts, one for each index of `groups`. A program takes and returns all parts, laid end to end along the dimension named above; each array names one. Nothing has to cross between parts.
Inputs may be any that keep to these rules, and one draw needn't show every extreme that they name: `footprint`: Real-valued sensitivities. `block_tile`: values are indices among the 32 swath tiles of the devices with the same bin and rep indices: owner value // 8 along rel, local tile value % 8. A device's list is grouped by owner in ascending order; at most 2 entries name one owner, and those name different tiles. In every group of devices with equal bin and rep indices, one owner is named 2 times by every device of the group.
All inputs are finite; a program needn't handle non-finite values. No bound on the sum of `pixel_mask` on one device may be relied on, other than what follows from the above.
Results may differ from a plain program's by a relative error of at most 0.002.
Values may be sent and summed in bfloat16 or wider, within the bound.
A program may use at most 64 MiB of HBM per device.

v0:
```python
import math

import jax
import jax.numpy as jnp
from jax import lax
from jax.sharding import PartitionSpec as P


def newton_update(gram_sum, gradient, release_part, mean_part, weight_part):
    slopes = jax.nn.sigmoid(release_part).T
    prior_diag = weight_part.T
    matrix = slopes[:, :, None] * gram_sum * slopes[:, None, :]
    matrix = 0.5 * (matrix + jnp.swapaxes(matrix, 1, 2))
    identity = jnp.eye(matrix.shape[1], dtype=jnp.float32)
    matrix = matrix + prior_diag[:, :, None] * identity[None]
    right_side = slopes * gradient - prior_diag * (release_part - mean_part).T
    factor = jnp.linalg.cholesky(matrix)
    partial_sol = jax.scipy.linalg.solve_triangular(factor, right_side[:, :, None], lower=True)
    update_step = jax.scipy.linalg.solve_triangular(factor, partial_sol, lower=True, trans=1)[
        :, :, 0
    ]
    return release_part + update_step.T


def body(
    footprint, block_tile, log_release, prior_mean, prior_weight, observed, noise_weight, pixel_mask
):
    blocks, releases, pixels = footprint.shape
    owners = lax.axis_size("rel")
    tile_count = observed.shape[0]
    bin_count = log_release.shape[1]
    capacity = blocks * 4 // 3 // owners
    slot_count = owners * capacity
    owner_ids = block_tile // tile_count
    positions = jnp.arange(blocks, dtype=jnp.int32)
    earlier = (owner_ids[:, None] == owner_ids[None, :]) & (positions[None, :] < positions[:, None])
    ranks = jnp.sum(earlier.astype(jnp.int32), axis=1)
    targets = owner_ids * capacity + ranks
    slot_match = targets[None, :] == jnp.arange(slot_count, dtype=jnp.int32)[:, None]
    slot_used = jnp.any(slot_match, axis=1)
    slot_source = jnp.sum(jnp.where(slot_match, positions[None, :], 0), axis=1)
    sent_tiles = jnp.where(slot_used, block_tile[slot_source] % tile_count, -1)
    recv_tile = lax.all_to_all(sent_tiles, "rel", split_axis=0, concat_axis=0, tiled=True)
    weight = pixel_mask[:, None, :].astype(jnp.float32) * noise_weight
    arrived = recv_tile >= 0
    picked = jnp.clip(recv_tile, 0, tile_count - 1)
    weight_slots = jnp.where(arrived[:, None, None], weight[picked], 0.0).astype(jnp.bfloat16)
    weight_back = lax.all_to_all(weight_slots, "rel", split_axis=0, concat_axis=0, tiled=True)
    rates = jax.nn.softplus(log_release).astype(jnp.bfloat16)
    outgoing = jnp.where(
        slot_used[:, None, None], footprint[slot_source], jnp.zeros((), jnp.bfloat16)
    )
    incoming = lax.all_to_all(outgoing, "rel", split_axis=0, concat_axis=0, tiled=True)
    rates_all = lax.all_gather(rates, "rel", axis=0, tiled=True)
    emission = jnp.einsum(
        "orb,ojrp->ojbp",
        rates_all.reshape(owners, releases, bin_count),
        incoming.reshape(owners, capacity, releases, pixels),
        preferred_element_type=jnp.float32,
    )
    emission = emission.reshape(slot_count, bin_count, pixels)
    tile_match = (recv_tile[None, :] == jnp.arange(tile_count, dtype=jnp.int32)[:, None]).astype(
        jnp.float32
    )
    predicted = jnp.dot(
        tile_match,
        emission.reshape(slot_count, bin_count * pixels),
        precision=lax.Precision.HIGHEST,
    )
    predicted = predicted.reshape(tile_count, bin_count, pixels)
    residual = weight * (observed - predicted)
    resid_slots = jnp.where(
        arrived[:, None, None], residual.astype(jnp.bfloat16)[picked], jnp.zeros((), jnp.bfloat16)
    )
    resid_back = lax.all_to_all(resid_slots, "rel", split_axis=0, concat_axis=0, tiled=True)
    resid_blocks = resid_back[targets]
    weight_blocks = weight_back[targets]
    gradient = jnp.einsum(
        "kbp,krp->br", resid_blocks, footprint, preferred_element_type=jnp.float32
    )
    group = math.gcd(blocks, 6)

    def add_group(counter, running):
        start = (counter * group).astype(jnp.int32)
        group_prints = lax.dynamic_slice_in_dim(footprint, start, group, 0)
        group_weights = lax.dynamic_slice_in_dim(weight_blocks, start, group, 0)
        scaled = (
            group_prints[:, None, :, :].astype(jnp.float32)
            * group_weights[:, :, None, :].astype(jnp.float32)
        ).astype(jnp.bfloat16)
        return running + jnp.einsum(
            "kbrp,ksp->brs", scaled, group_prints, preferred_element_type=jnp.float32
        )

    gram_sum = lax.fori_loop(
        0, blocks // group, add_group, jnp.zeros((bin_count, releases, releases), jnp.float32)
    )
    planes = lax.axis_size(("bin", "rep"))
    share = bin_count // planes
    first_bin = lax.axis_index(("bin", "rep")) * share
    gram_all, grad_all = lax.psum((gram_sum, gradient), ("bin", "rep"))
    gram_own = lax.dynamic_slice_in_dim(gram_all, first_bin, share, 0)
    grad_own = lax.dynamic_slice_in_dim(grad_all, first_bin, share, 0)

    def take_bins(array):
        return lax.dynamic_slice_in_dim(array, first_bin, share, 1)

    release_new = newton_update(
        gram_own, grad_own, take_bins(log_release), take_bins(prior_mean), take_bins(prior_weight)
    )
    return (release_new, residual)


def solution(mesh):
    in_specs = (
        P(("groups", "rel", "bin", "rep"), None, None),
        P(("groups", "rel", "bin", "rep")),
        P(("groups", "rel"), None),
        P(("groups", "rel"), None),
        P(("groups", "rel"), None),
        P(("groups", "rel", "bin", "rep"), None, None),
        P(("groups", "rel", "bin", "rep"), None, None),
        P(("groups", "rel", "bin", "rep"), None),
    )
    out_specs = (
        P(("groups", "rel"), ("bin", "rep")),
        P(("groups", "rel", "bin", "rep"), None, None),
    )
    return jax.shard_map(body, mesh=mesh, in_specs=in_specs, out_specs=out_specs, check_vma=False)
```

profile of v0, /device:TPU:0, one launch (start us, length us, event | category | flops | bytes accessed | tf_op | source)
XLA Modules:
  0.0 295.2 jit_solution(6431508337299272755)
XLA Ops:
  7.2 0.7 and_select_fusion
  7.9 0.2 convert_reduce_fusion
  8.1 0.7 compare_select_fusion.1
  8.7 0.1 fusion.18
  8.9 0.1 select_reduce_fusion.1
  9.0 0.1 reduce_or.12
  9.1 1.3 gather_fusion
  10.5 0.6 fusion.23
  11.1 6.3 %all-to-all-start = ((s32[4,2,1]{1,2,0:T(1,128)}), s32[4,2,1]{1,2,0:T(1,128)S(1)}, u32[]{:S(2)}, u32[]{:S(2)}) async-start(s32[4,2,1]{1,2,0:T(1,128)} %bitcast.3), calls=%async_computation | async-start | bytes 4096 | tf_op jit(solution)/shard_map/all_to_all | solution.py:43
  17.4 1.5 gather_fusion.3
  18.9 1.0 convert_element_type.42
  19.9 0.7 convert_element_type.44
  20.6 1.0 copy_multiply_fusion
  21.7 0.8 broadcast_select_fusion
  22.5 12.4 %all_gather.3 = bf16[512,32]{0,1:T(8,128)(2,1)S(1)} all-gather(bf16[128,32]{0,1:T(8,128)(2,1)S(1)} %fusion.16), channel_id=1, replica_groups=mesh['groups'=2,'rel'=4,'bin'=2,'rep'=2] {'rel'}, dimensions={0}, use_global_device_ids=true | all-gather | bytes 40960 | tf_op jit(solution)/shard_map/all_gather | solution.py:54
  34.9 3.4 %all-to-all-start.2 = ((bf16[8,128,128]{2,1,0:T(8,128)(2,1)}), bf16[8,128,128]{2,1,0:T(8,128)(2,1)S(1)}, u32[]{:S(2)}, u32[]{:S(2)}) async-start(bf16[8,128,128]{2,1,0:T(8,128)(2,1)} %broadcast_select_fusion), calls=%async_computation.2 | async-start | bytes 524288 | tf_op jit(solution)/shard_map/all_to_all | solution.py:53
  38.4 0.5 broadcast.249
  39.0 0.7 reduce.9
  39.6 0.1 all_to_all.16
  39.7 0.6 gather_fusion.1
  40.3 4.8 %all-to-all-done.2 = bf16[8,128,128]{2,1,0:T(8,128)(2,1)S(1)} async-done(((bf16[8,128,128]{2,1,0:T(8,128)(2,1)}), bf16[8,128,128]{2,1,0:T(8,128)(2,1)S(1)}, u32[]{:S(2)}, u32[]{:S(2)}) %all-to-all-start.2) | async-done | bytes 262176 | tf_op jit(solution)/shard_map/all_to_all | solution.py:53
  45.1 0.2 fusion.13
  45.2 0.3 fusion.27
  45.5 0.6 gather_fusion.4
  46.1 0.8 select_convert_fusion
  46.9 3.4 %all-to-all-start.1 = ((bf16[8,32,128]{2,1,0:T(8,128)(2,1)}), bf16[8,32,128]{2,1,0:T(8,128)(2,1)S(1)}, u32[]{:S(2)}, u32[]{:S(2)}) async-start(bf16[8,32,128]{2,1,0:T(8,128)(2,1)} %get-tuple-element.27), calls=%async_computation.1 | async-start | bytes 131072 | tf_op jit(solution)/shard_map/all_to_all | solution.py:48
  50.3 5.7 %all-to-all-done.1 = bf16[8,32,128]{2,1,0:T(8,128)(2,1)S(1)} async-done(((bf16[8,32,128]{2,1,0:T(8,128)(2,1)}), bf16[8,32,128]{2,1,0:T(8,128)(2,1)S(1)}, u32[]{:S(2)}, u32[]{:S(2)}) %all-to-all-start.1) | async-done | bytes 65568 | tf_op jit(solution)/shard_map/all_to_all | solution.py:48
  56.0 0.6 gather_fusion.2
  56.6 3.5 %fusion.3 = f32[32,128,128]{1,2,0:T(8,128)} fusion(f32[6,32,128]{2,0,1:T(8,128)S(1)} %copy.42, f32[6,128,128]{2,1,0:T(8,128)S(1)} %convert_element_type.42, bf16[6,128,128]{2,1,0:T(8,128)(2,1)S(1)} %copy-done), kind=kOutput, calls=%fused_computation.10 | convolution fusion | flops 811597824 | bytes 2785280 | tf_op jit(solution)/shard_map/while/body/eval_jaxpr/kbrp,ksp->brs/dot_general | solution.py:91
  60.2 3.3 %all-to-all-start.3 = ((bf16[8,32,128]{2,1,0:T(8,128)(2,1)}), bf16[8,32,128]{2,1,0:T(8,128)(2,1)S(1)}, u32[]{:S(2)}, u32[]{:S(2)}) async-start(bf16[8,32,128]{2,1,0:T(8,128)(2,1)} %get-tuple-element.28), calls=%async_computation.3 | async-start | bytes 131072 | tf_op jit(solution)/shard_map/all_to_all | solution.py:75
  63.5 0.7 copy.49
  64.2 5.0 %all-to-all-done.3 = bf16[8,32,128]{2,1,0:T(8,128)(2,1)S(1)} async-done(((bf16[8,32,128]{2,1,0:T(8,128)(2,1)}), bf16[8,32,128]{2,1,0:T(8,128)(2,1)S(1)}, u32[]{:S(2)}, u32[]{:S(2)}) %all-to-all-start.3) | async-done | bytes 65568 | tf_op jit(solution)/shard_map/all_to_all | solution.py:75
  69.2 0.6 gather_fusion.5
  69.8 0.1 convolution_bitcast_fusion
  69.9 12.0 %psum.15 = f32[32,128]{1,0:T(8,128)S(1)} all-reduce(f32[32,128]{1,0:T(8,128)S(1)} %convolution_bitcast_fusion), channel_id=1, replica_groups=mesh['groups'=2,'rel'=4,'bin'=2,'rep'=2] {'bin','rep'}, use_global_device_ids=true, to_apply=%region_6.7 | all-reduce | flops 4096 | bytes 32768 | tf_op jit(solution)/shard_map/psum | solution.py:101
  81.9 0.7 fusion.17
  82.6 27.9 %all-reduce.2.cloned.1.call-done = f32[32,128,128]{1,2,0:T(8,128)} async-done(((f32[32,128,128]{1,2,0:T(8,128)}), f32[32,128,128]{1,2,0:T(8,128)}) %all-reduce.2.cloned.1.call-update) | async-done | bytes 2097168 | tf_op jit(solution)/shard_map/psum | solution.py:101
  110.5 1.2 multiply_multiply_fusion
  111.7 0.2 copy.44
  111.9 1.4 fusion.10
  113.3 0.2 copy.45
  113.6 93.8 %custom-call.11 = f32[8,128,128]{2,1,0:T(8,128)S(1)} custom-call(f32[8,128,128]{2,1,0:T(8,128)S(1)} %fusion.8), custom_call_target="Cholesky" | custom-call | tf_op jit(solution)/shard_map/jit(cholesky)/cholesky | solution.py:17
  207.4 0.1 compare_reduce_fusion
  207.6 0.1 select_bitcast_fusion
  207.7 78.6 %custom-call.12 = f32[8,1,128,128]{2,3,1,0:T(8,128)S(1)} custom-call(f32[8,1,128,128]{3,2,1,0:T(8,128)S(1)} %select_bitcast_fusion), custom_call_target="InvertDiagBlocksLowerTriangular" | custom-call | tf_op jit(solution)/shard_map/jit(_solve_triangular)/vmap()/triangular_solve | solution.py:19
  286.3 0.6 convolution_bitcast_fusion.1
  286.8 0.9 fusion.5
  287.8 0.6 dynamic-slice_add_fusion
  (32 shorter events, 0.5 us)
Async XLA Ops:
  7.2 15.3 %copy-start.2 = (f32[128,32]{0,1:T(8,128)S(1)}, f32[128,32]{0,1:T(8,128)}, u32[]{:S(2)}) copy-start(f32[128,32]{0,1:T(8,128)} %param.10) | copy-start | bytes 49156
  7.2 38.1 %copy-start.1 = (f32[8,32,128]{2,1,0:T(8,128)S(1)}, f32[8,32,128]{2,1,0:T(8,128)}, u32[]{:S(2)}) copy-start(f32[8,32,128]{2,1,0:T(8,128)} %param.13) | copy-start | bytes 393220
  11.1 23.8 %all-to-all-start = ((s32[4,2,1]{1,2,0:T(1,128)}), s32[4,2,1]{1,2,0:T(1,128)S(1)}, u32[]{:S(2)}, u32[]{:S(2)}) async-start(s32[4,2,1]{1,2,0:T(1,128)} %bitcast.3), calls=%async_computation | async-start | bytes 4096 | tf_op jit(solution)/shard_map/all_to_all | solution.py:43
  18.9 37.7 %copy-start = (bf16[6,128,128]{2,1,0:T(8,128)(2,1)S(1)}, bf16[6,128,128]{2,1,0:T(8,128)(2,1)}, u32[]{:S(2)}) copy-start(bf16[6,128,128]{2,1,0:T(8,128)(2,1)} %param.8) | copy-start | bytes 589828
  34.9 10.2 %all-to-all-start.2 = ((bf16[8,128,128]{2,1,0:T(8,128)(2,1)}), bf16[8,128,128]{2,1,0:T(8,128)(2,1)S(1)}, u32[]{:S(2)}, u32[]{:S(2)}) async-start(bf16[8,128,128]{2,1,0:T(8,128)(2,1)} %broadcast_select_fusion), calls=%async_computation.2 | async-start | bytes 524288 | tf_op jit(solution)/shard_map/all_to_all | solution.py:53
  46.9 9.2 %all-to-all-start.1 = ((bf16[8,32,128]{2,1,0:T(8,128)(2,1)}), bf16[8,32,128]{2,1,0:T(8,128)(2,1)S(1)}, u32[]{:S(2)}, u32[]{:S(2)}) async-start(bf16[8,32,128]{2,1,0:T(8,128)(2,1)} %get-tuple-element.27), calls=%async_computation.1 | async-start | bytes 131072 | tf_op jit(solution)/shard_map/all_to_all | solution.py:48
  50.3 60.2 %all-reduce.2.cloned.1.call-start = ((), (), s32[]{:S(2)}) async-start(), calls=%async_computation.4 | async-start | bytes 4194304 | tf_op jit(solution)/shard_map/psum | solution.py:101
  60.1 3.4 %copy-start.3 = (f32[128,32]{0,1:T(8,128)S(1)}, f32[128,32]{0,1:T(8,128)}, u32[]{:S(2)}) copy-start(f32[128,32]{0,1:T(8,128)} %param.12) | copy-start | bytes 49156
  60.2 9.0 %all-to-all-start.3 = ((bf16[8,32,128]{2,1,0:T(8,128)(2,1)}), bf16[8,32,128]{2,1,0:T(8,128)(2,1)S(1)}, u32[]{:S(2)}, u32[]{:S(2)}) async-start(bf16[8,32,128]{2,1,0:T(8,128)(2,1)} %get-tuple-element.28), calls=%async_computation.3 | async-start | bytes 131072 | tf_op jit(solution)/shard_map/all_to_all | solution.py:75
Sparse Core Ops, SparseCore 0:
  60.2 50.2 all-reduce.1
where the time goes:
time: 296 us; the launch traced here: 295 us
  other arithmetic  184 us (62%)
  waiting for transfers between devices  43.4 us (15%)
  blocking collectives  24.4 us (8%)
  starting transfers between devices  16.5 us (6%)
  between operations  14.3 us (5%)
  local copies, waits for them, and re-layouts  7.09 us (2%)
  matrix products  5.49 us (2%)
    another operation x4, other arithmetic, newton_update(): factor = jnp.linalg.cholesky(matrix)  94 us
    another operation x3, other arithmetic, newton_update(): jax.scipy.linalg.solve_triangular(factor, partial_sol, lower=True, trans=1)  78.7 us
    psum x1, waiting for transfers between devices, body(): gram_all, grad_all = lax.psum((gram_sum, gradient), ('bin', 'rep'))  27.9 us
    all_gather x1, blocking collectives, body(): rates_all = lax.all_gather(rates, 'rel', axis=0, tiled=True)  12.4 us
    psum x1, blocking collectives, body(): gram_all, grad_all = lax.psum((gram_sum, gradient), ('bin', 'rep'))  12 us
    all_to_all x1, starting transfers between devices, body(): lax.all_to_all(sent_tiles, 'rel', split_axis=0, concat_axis=0, tiled=True)  6.32 us
  transfers between devices with their start and end apart: 5, of which 4 were waited for; matrix products, arithmetic and copies ran while one was open for 3% of the time, Pallas kernels for 0%

commit v1 on v0

v1 whole, which is shorter than its diff:
```python
import functools
import math

import jax
import jax.numpy as jnp
from jax import lax
from jax.experimental import pallas as pl
from jax.experimental.pallas import tpu as pltpu
from jax.sharding import PartitionSpec as P

MESH = pl.DeviceIdType.MESH
F32, BF16 = jnp.float32, jnp.bfloat16
HIGHEST = lax.Precision.HIGHEST
NN = (((1,), (0,)), ((), ()))
TN = (((0,), (0,)), ((), ()))
PANEL = 32


def dot(a, b, dims=NN, precision=None):
    return lax.dot_general(a, b, dims, precision=precision, preferred_element_type=F32)


def split(x):
    high = x.astype(BF16)
    rest = x - high.astype(F32)
    middle = rest.astype(BF16)
    return high, middle, (rest - middle.astype(F32)).astype(BF16)


def step_kernel(
    owners, xs, share, cap,
    fp_hbm, bt, lr_hbm, mean_hbm, pw_hbm, obs_hbm, noise_hbm, mask_hbm,
    resid_hbm, updated,
    fp, far, obs, noise, resid, lr, mean, pw, mask,
    idx_send, idx_recv, w_send, w_recv, em_send, em_recv, r_send, r_recv,
    weight, ft, w_out, w_in, r_out, r_in, wrows,
    mat, pan,
    in_s, out_s,
    idx_ss, idx_rs, w_ss, w_rs, em_ss, em_rs, r_ss, r_rs,
    wp_ss, wp_rs, rp_ss, rp_rs, fp_ss, fp_rs,
):
    blocks, releases, pixels = fp.shape
    planes = 2 * xs
    tiles, bins, _ = obs.shape
    half = blocks // 2
    pack = 16 // share
    me, mx, mc = lax.axis_index("rel"), lax.axis_index("bin"), lax.axis_index("rep")

    def rel_id(step):
        return {"rel": lax.rem(me + step, owners)}

    def plane_id(dx, dc):
        return {"bin": lax.rem(mx + dx, xs), "rep": lax.rem(mc + dc, 2)}

    others = [(dx, dc) for dx in range(xs) for dc in range(2) if (dx, dc) != (0, 0)]

    def remote(src, dst, ss, rs, target):
        return pltpu.make_async_remote_copy(
            src_ref=src, dst_ref=dst, send_sem=ss, recv_sem=rs, device_id=target,
            device_id_type=MESH,
        )

    loads = [
        pltpu.make_async_copy(src, dst, in_s.at[n])
        for n, (src, dst) in enumerate((
            (lr_hbm, lr), (fp_hbm, fp), (mask_hbm, mask), (noise_hbm, noise), (obs_hbm, obs),
            (mean_hbm, mean), (pw_hbm, pw),
        ))
    ]
    for copy in loads:
        copy.start()
    barrier = pltpu.get_barrier_semaphore()
    for step in range(1, owners):
        pl.semaphore_signal(barrier, inc=1, device_id=rel_id(step), device_id_type=MESH)
    for dx, dc in others:
        pl.semaphore_signal(barrier, inc=1, device_id=plane_id(dx, dc), device_id_type=MESH)

    sub = lax.broadcasted_iota(jnp.int32, (8, pixels), 0)
    slots = {}
    for step in range(owners):
        first_tile = lax.rem(me + step, owners) * tiles
        start, end = jnp.int32(0), jnp.int32(0)
        for k in range(blocks):
            start += (bt[k] < first_tile).astype(jnp.int32)
            end += (bt[k] < first_tile + tiles).astype(jnp.int32)
        table = jnp.full((8, pixels), -1, jnp.int32)
        for j in range(cap):
            source = jnp.minimum(start + j, blocks - 1)
            used = start + j < end
            tile = jnp.where(used, bt[source] - first_tile, -1)
            slots[step, j] = source, used
            table = jnp.where(sub == j, tile, table)
        if step:
            idx_send[step] = table
        else:
            idx_recv[0] = table

    pl.semaphore_wait(barrier, owners - 1 + len(others))
    idx_copies = [
        remote(idx_send.at[s], idx_recv.at[s], idx_ss.at[s], idx_rs.at[s], rel_id(s))
        for s in range(1, owners)
    ]
    for copy in idx_copies:
        copy.start()
    piece = [pl.ds(h * half, half) for h in range(2)]
    across, over = {}, {}
    for h in range(2):
        for dx in range(1, xs):
            across[dx, h] = remote(
                fp_hbm.at[piece[h]], far.at[2 * dx, piece[h]],
                fp_ss.at[2 * dx, h], fp_rs.at[2 * dx, h], plane_id(dx, 0),
            )
            across[dx, h].start()
        over[0, h] = remote(
            fp_hbm.at[piece[h]], far.at[1, piece[h]], fp_ss.at[1, h], fp_rs.at[1, h],
            plane_id(0, 1),
        )
        over[0, h].start()

    loads[0].wait()
    rates = jnp.log1p(jnp.exp(-jnp.abs(lr[...]))) + jnp.maximum(lr[...], 0.0)
    rates = rates.astype(BF16)
    loads[1].wait()
    em_copies = []
    for step in [*range(1, owners), 0]:
        target = em_send if step else em_recv
        for j in range(cap):
            source, used = slots[step, j]
            emission = dot(rates, fp[source])
            target[step, j] = jnp.where(used, emission, 0.0)
        if step:
            copy = remote(
                em_send.at[step], em_recv.at[step], em_ss.at[step], em_rs.at[step], rel_id(step)
            )
            copy.start()
            em_copies.append(copy)

    loads[2].wait()
    loads[3].wait()
    for t in range(tiles):
        weight[t] = mask[t : t + 1, :].astype(F32) * noise[t]

    def turn(slot):
        blocks_here = far.at[slot] if slot else fp
        for k in range(blocks):
            ft[slot, k * pixels : (k + 1) * pixels, :] = blocks_here[k].T

    turn(0)

    back_ids = [rel_id(owners - s) for s in range(owners)]

    def pick(step, j, array):
        row = idx_recv[step][j : j + 1, :]
        total = jnp.zeros(array.shape[1:], F32)
        for t in range(tiles):
            total = jnp.where(row == t, array[t], total)
        return total.astype(BF16)

    w_copies = []
    for step in [*range(1, owners), 0]:
        if step:
            idx_copies[step - 1].wait_recv()
        target = w_send if step else w_recv
        for j in range(cap):
            target[step, j] = pick(step, j, weight)
        if step:
            copy = remote(
                w_send.at[step], w_recv.at[step], w_ss.at[step], w_rs.at[step], back_ids[step]
            )
            copy.start()
            w_copies.append(copy)
    loads[4].wait()
    for copy in em_copies:
        copy.wait_recv()
    for t in range(tiles):
        total = jnp.zeros((bins, pixels), F32)
        for step in range(owners):
            for j in range(cap):
                row = idx_recv[step][j : j + 1, :]
                total += jnp.where(row == t, em_recv[step, j], 0.0)
        resid[t] = weight[t] * (obs[t] - total)
    resid_out = pltpu.make_async_copy(resid, resid_hbm, out_s)
    resid_out.start()
    r_copies = []
    for step in [*range(1, owners), 0]:
        target = r_send if step else r_recv
        for j in range(cap):
            target[step, j] = pick(step, j, resid)
        if step:
            copy = remote(
                r_send.at[step], r_recv.at[step], r_ss.at[step], r_rs.at[step], back_ids[step]
            )
            copy.start()
            r_copies.append(copy)

    for dx in range(1, xs):
        for h in range(2):
            across[dx, h].wait_recv()
            over[dx, h] = remote(
                far.at[2 * dx, piece[h]], far.at[2 * dx + 1, piece[h]],
                fp_ss.at[2 * dx + 1, h], fp_rs.at[2 * dx + 1, h], plane_id(0, 1),
            )
            over[dx, h].start()

    places = []
    for k in range(blocks):
        owner = bt[k] // tiles
        rank = jnp.int32(0)
        for back in range(1, cap):
            if k - back >= 0:
                rank += (bt[k - back] // tiles == owner).astype(jnp.int32)
        places.append((lax.rem(owner - me + owners, owners), rank))

    def to_plane(array, out, arrived, ss, rs):
        for k in range(0, blocks, pack):
            rows = [array[place].astype(F32) for place in places[k : k + pack]]
            for q in range(planes):
                wanted = [row[q * share : (q + 1) * share] for row in rows]
                wanted = jnp.concatenate(wanted, axis=0).astype(BF16)
                out[q, k * share : (k + pack) * share, :] = wanted
        copies = []
        for dx, dc in others:
            target, slot = plane_id(dx, dc), 2 * dx + dc
            copy = remote(
                out.at[target["bin"] * 2 + target["rep"]], arrived.at[slot],
                ss.at[slot], rs.at[slot], target,
            )
            copy.start()
            copies.append(copy)
        return copies

    here = mx * 2 + mc
    for copy in w_copies:
        copy.wait_recv()
    wp_copies = to_plane(w_recv, w_out, w_in, wp_ss, wp_rs)

    group = math.gcd(blocks, 6)

    def gram(slot, fresh):
        blocks_here = far.at[slot] if slot else fp

        def add(start):
            def pair(i, carry):
                rows = []
                for b in range(2):
                    parts = []
                    for n in range(group):
                        w = wrows[pl.ds((start + n) * share + 2 * i + b, 1), :]
                        parts.append(blocks_here[start + n] * w.astype(BF16))
                    rows.append(jnp.concatenate(parts, axis=1))
                turned = ft[slot, pl.ds(pl.multiple_of(start * pixels, 128), group * pixels), :]
                total = dot(jnp.concatenate(rows, axis=0), turned)
                for b in range(2):
                    part = total[b * releases : (b + 1) * releases]
                    mat[2 * i + b] = part if fresh else mat[2 * i + b] + part
                return carry

            lax.fori_loop(0, share // 2, pair, 0)

        if blocks == group:
            add(0)
        else:
            if fresh:
                mat[...] = jnp.zeros_like(mat)
            fresh = False
            lax.fori_loop(0, blocks // group, lambda g, c: (add(g * group), c)[1], 0)

    wrows[...] = w_out[here].astype(F32)
    gram(0, True)

    for copy in r_copies:
        copy.wait_recv()
    rp_copies = to_plane(r_recv, r_out, r_in, rp_ss, rp_rs)

    for n, (dx, dc) in enumerate(others):
        slot = 2 * dx + dc
        for h in range(2):
            if dc:
                over[dx, h].wait_recv()
        wp_copies[n].wait_recv()
        turn(slot)
        wrows[...] = w_in[slot].astype(F32)
        gram(slot, False)

    loads[5].wait()
    loads[6].wait()
    first = (mx * 2 + mc) * share
    want = lax.broadcasted_iota(jnp.int32, (share, bins), 0) + first
    chosen = (lax.broadcasted_iota(jnp.int32, (share, bins), 1) == want).astype(F32)
    lr_t, mean_t, pw_t = (dot(chosen, ref[...], NN, HIGHEST) for ref in (lr, mean, pw))
    inverse_slope = 1.0 + jnp.exp(-lr_t)
    extra = pw_t * inverse_slope * inverse_slope

    row_id = lax.broadcasted_iota(jnp.int32, (releases, releases), 0)
    col_id = lax.broadcasted_iota(jnp.int32, (releases, releases), 1)
    on = row_id == col_id
    for b in range(share):
        square = mat[b]
        square = 0.5 * (square + square.T)
        mat[b] = jnp.where(on, square + extra[b : b + 1], square)

    invert(share, mat, pan)

    def side(array):
        wide = array.astype(F32)
        parts = [wide[k * share : (k + 1) * share] for k in range(blocks)]
        return jnp.concatenate(parts, axis=1).astype(BF16)

    total = dot(side(r_out[here]), ft[0])
    for n, (dx, dc) in enumerate(others):
        rp_copies[n].wait_recv()
        total += dot(side(r_in[2 * dx + dc]), ft[2 * dx + dc])
    right = total - pw_t * (lr_t - mean_t) * inverse_slope
    wide = jnp.concatenate([*split(right), jnp.zeros_like(right, BF16)], axis=0)
    sub_share = lax.broadcasted_iota(jnp.int32, (share, releases), 0)
    change = jnp.zeros((share, releases), F32)
    for b in range(share):
        high, middle, low = (dot(wide, part) for part in split(mat[b]))
        solved = (
            high[:share] + high[share : 2 * share] + high[2 * share : 3 * share]
            + middle[:share] + middle[share : 2 * share] + low[:share]
        )
        change = jnp.where(sub_share == b, solved, change)
    updated[...] = lr_t + change * inverse_slope

    for copy in [
        *idx_copies, *em_copies, *w_copies, *r_copies, *wp_copies, *rp_copies,
        *across.values(), *over.values(),
    ]:
        copy.wait_send()
    resid_out.wait()


def invert(share, mat, pan):
    releases = mat.shape[1]
    lane = lax.broadcasted_iota(jnp.int32, (share, releases), 1)
    col_id = lax.broadcasted_iota(jnp.int32, (releases, releases), 1)
    panel_lane = lax.broadcasted_iota(jnp.int32, (PANEL, releases), 1)
    for base in range(0, releases, PANEL):
        for b in range(share):
            pan[pl.ds(b, PANEL, stride=share), :] = mat[b, base : base + PANEL, :]
        rows = pan[...].reshape(PANEL, share, releases)
        for k in range(0, PANEL, 2):
            c = base + k
            f0 = jnp.broadcast_to(rows[:, :, c : c + 1], rows.shape)
            f1 = jnp.broadcast_to(rows[:, :, c + 1 : c + 2], rows.shape)
            p, q, r, s = f0[k], f1[k], f0[k + 1], f1[k + 1]
            scale = 1.0 / (p * s - q * r)
            at0, at1 = lane == c, lane == c + 1
            u0 = jnp.where(at0, 1.0, jnp.where(at1, 0.0, rows[k]))
            u1 = jnp.where(at1, 1.0, jnp.where(at0, 0.0, rows[k + 1]))
            n0 = (s * u0 - q * u1) * scale
            n1 = (p * u1 - r * u0) * scale
            pivots = jnp.concatenate([n0[None], n1[None]], axis=0)
            gone = (at0 | at1)[None]

            def reduce(a, z):
                kept = jnp.where(gone, 0.0, rows[a:z])
                return kept - f0[a:z] * n0[None] - f1[a:z] * n1[None]

            pieces = [reduce(0, k)] if k else []
            pieces.append(pivots)
            if k + 2 < PANEL:
                pieces.append(reduce(k + 2, PANEL))
            rows = jnp.concatenate(pieces, axis=0)
        pan[...] = rows.reshape(PANEL * share, releases)
        inside = (col_id >= base) & (col_id < base + PANEL)
        for b in range(share):
            old = mat[b]
            side = old[base : base + PANEL]
            side = jnp.where(panel_lane < base, -side, side)
            new = pan[pl.ds(b, PANEL, stride=share), :]
            sh, sm, sl = split(side)
            nh, nm, nl = split(new)
            left = jnp.concatenate([sh, sh, sm, sh, sl, sm], axis=0)
            right = jnp.concatenate([nh, nm, nh, nl, nh, nm], axis=0)
            moved = jnp.where(inside, 0.0, old) - dot(left, right, TN)
            mat[b] = moved
            mat[b, base : base + PANEL, :] = new


def body(
    footprint, block_tile, log_release, prior_mean, prior_weight, observed, noise_weight, pixel_mask
):
    blocks, releases, pixels = footprint.shape
    tiles, bins, _ = observed.shape
    owners, xs = lax.axis_size("rel"), lax.axis_size("bin")
    cap = blocks * 4 // 3 // owners
    planes = 2 * xs
    share = bins // planes
    vmem = pl.BlockSpec(memory_space=pltpu.VMEM)
    smem = pl.BlockSpec(memory_space=pltpu.SMEM)
    dma = pltpu.SemaphoreType.DMA
    slot = (owners, cap, bins, pixels)
    rows = (planes, blocks * share, pixels)
    hbm = pl.BlockSpec(memory_space=pltpu.HBM)
    residual, updated = pl.pallas_call(
        functools.partial(step_kernel, owners, xs, share, cap),
        out_shape=(
            jax.ShapeDtypeStruct(observed.shape, F32),
            jax.ShapeDtypeStruct((share, releases), F32),
        ),
        in_specs=[hbm, smem, hbm, hbm, hbm, hbm, hbm, hbm],
        out_specs=(hbm, vmem),
        scratch_shapes=[
            pltpu.VMEM(footprint.shape, BF16),
            pltpu.VMEM((planes, *footprint.shape), BF16),
            *[pltpu.VMEM(observed.shape, F32) for _ in range(3)],
            *[pltpu.VMEM((bins, releases), F32) for _ in range(3)],
            pltpu.VMEM((tiles, pixels), jnp.int32),
            pltpu.VMEM((owners, 8, pixels), jnp.int32),
            pltpu.VMEM((owners, 8, pixels), jnp.int32),
            pltpu.VMEM(slot, BF16), pltpu.VMEM(slot, BF16),
            pltpu.VMEM(slot, F32), pltpu.VMEM(slot, F32),
            pltpu.VMEM(slot, BF16), pltpu.VMEM(slot, BF16),
            pltpu.VMEM(observed.shape, F32),
            pltpu.VMEM((planes, blocks * pixels, releases), BF16),
            *[pltpu.VMEM(rows, BF16) for _ in range(4)],
            pltpu.VMEM(rows[1:], F32),
            pltpu.VMEM((share, releases, releases), F32),
            pltpu.VMEM((PANEL * share, releases), F32),
            dma((7,)), dma,
            *[dma((owners,)) for _ in range(8)],
            *[dma((planes,)) for _ in range(4)],
            dma((planes, 2)), dma((planes, 2)),
        ],
        compiler_params=pltpu.CompilerParams(
            collective_id=0, has_side_effects=True, vmem_limit_bytes=60 * 2**20
        ),
        name="newton_step",
    )(
        footprint, block_tile, log_release.T, prior_mean.T, prior_weight.T, observed,
        noise_weight, pixel_mask,
    )
    return (updated.T, residual)


def solution(mesh):
    in_specs = (
        P(("groups", "rel", "bin", "rep"), None, None),
        P(("groups", "rel", "bin", "rep")),
        P(("groups", "rel"), None),
        P(("groups", "rel"), None),
        P(("groups", "rel"), None),
        P(("groups", "rel", "bin", "rep"), None, None),
        P(("groups", "rel", "bin", "rep"), None, None),
        P(("groups", "rel", "bin", "rep"), None),
    )
    out_specs = (
        P(("groups", "rel"), ("bin", "rep")),
        P(("groups", "rel", "bin", "rep"), None, None),
    )
    return jax.shard_map(body, mesh=mesh, in_specs=in_specs, out_specs=out_specs, check_vma=False)
```

time: 296 us -> 33.8 us (0.11)
  other arithmetic: 184 us -> 0 us
  waiting for transfers between devices: 43.4 us -> 0 us
  Pallas kernels: 0 us -> 30.1 us
  blocking collectives: 24.4 us -> 0 us
  starting transfers between devices: 16.5 us -> 0 us
  between operations: 14.3 us -> 0.65 us
  matrix products: 5.49 us -> 0 us
  local copies, waits for them, and re-layouts: 7.09 us -> 2.82 us
    another operation x7 -> x0, other arithmetic: 173 us -> none  [the longest x4 94 us: newton_update(): factor = jnp.linalg.cholesky(matrix)]
    pallas_call x0 -> x1, Pallas kernels: none -> 30.1 us  [body(): pl.pallas_call(functools.partial(step_kernel, owners, xs, share, cap), ou...]
    psum x1 -> x0, waiting for transfers between devices: 27.9 us -> none  [body(): gram_all, grad_all = lax.psum((gram_sum, gradient), ('bin', 'rep'))]
    all_to_all x4 -> x0, starting transfers between devices: 16.5 us -> none  [the longest x1 6.32 us: body(): lax.all_to_all(sent_tiles, 'rel', split_axis=0, concat_axis=0, tiled=True)]
    all_to_all x4 -> x0, waiting for transfers between devices: 15.5 us -> none  [the longest x1 5.73 us: body(): lax.all_to_all(weight_slots, 'rel', split_axis=0, concat_axis=0, tiled=True)]
    all_gather x1 -> x0, blocking collectives: 12.4 us -> none  [body(): rates_all = lax.all_gather(rates, 'rel', axis=0, tiled=True)]
    psum x1 -> x0, blocking collectives: 12 us -> none  [body(): gram_all, grad_all = lax.psum((gram_sum, gradient), ('bin', 'rep'))]
    gather x7 -> x0, local copies, waits for them, and re-layouts: 5.15 us -> none  [the longest x1 1.52 us: body(): footprint[slot_source]]
  transfers between devices with their start and end apart: 5 -> 0, of which waited for: 4 -> 0; matrix products, arithmetic and copies ran while one was open for 3% -> 0% of each run, Pallas kernels for 0% -> 0%
where the time goes in v1:
time: 33.8 us; the launch traced here: 33.6 us
  Pallas kernels  30.1 us (89%)
  local copies, waits for them, and re-layouts  2.82 us (8%)
  between operations  0.65 us (2%)
    pallas_call x1, Pallas kernels, body(): pl.pallas_call(functools.partial(step_kernel, owners, xs, share, cap), ou...  30.1 us
    unnamed x4, local copies, waits for them, and re-layouts  2.82 us

profile of v1, /device:TPU:0, one launch (start us, length us, event | category | flops | bytes accessed | tf_op | source)
XLA Modules:
  0.0 33.6 jit_solution(11173603809265021955)
XLA Ops:
  0.6 30.1 %newton_step.1 = (f32[8,32,128]{2,1,0:T(8,128)}, f32[8,128]{1,0:T(8,128)}) custom-call(bf16[6,128,128]{2,1,0:T(8,128)(2,1)} %fp_hbm.1, s32[6]{0:T(128)} %bt.1, f32[32,128]{1,0:T(8,128)} %bitcast.4, f32[32,128]{1,0:T(8,128)} %bitcast.5, f32[32,128]{1,0:T(8,128)} %bitcast.6, f32[8,32,128]{2,1,0:T(8,128)} %obs_hbm.1, f32[8,32,128]{2,1,0:T(8,128)} %noise_hbm.1, ...), custom_call_target="tpu_custom_call" | custom-call | tf_op jit(solution)/shard_map/newton_step/pallas_call | solution.py:397
  30.8 0.0 copy-start
  30.8 0.7 %copy-done = f32[8,128]{1,0:T(8,128)S(1)} copy-done((f32[8,128]{1,0:T(8,128)S(1)}, f32[8,128]{1,0:T(8,128)}, u32[]{:S(2)}) %copy-start) | copy-done | bytes 4120
  31.5 0.6 %copy.12 = f32[128,8]{0,1:T(8,128)} copy(f32[128,8]{0,1:T(8,128)S(1)} %bitcast.7) | data formatting | bytes 8192
  32.0 1.6 %copy.13 = f32[8,32,128]{2,1,0:T(8,128)} copy(f32[8,32,128]{2,1,0:T(8,128)} %get-tuple-element.9) | data formatting | bytes 262144
Async XLA Ops:
  30.8 0.7 %copy-start = (f32[8,128]{1,0:T(8,128)S(1)}, f32[8,128]{1,0:T(8,128)}, u32[]{:S(2)}) copy-start(f32[8,128]{1,0:T(8,128)} %get-tuple-element.4) | copy-start | bytes 12292

commit v2 on v1

--- a/solution.py
+++ b/solution.py
@@ -10,14 +10,13 @@
 
 MESH = pl.DeviceIdType.MESH
 F32, BF16 = jnp.float32, jnp.bfloat16
-HIGHEST = lax.Precision.HIGHEST
 NN = (((1,), (0,)), ((), ()))
 TN = (((0,), (0,)), ((), ()))
 PANEL = 32
 
 
-def dot(a, b, dims=NN, precision=None):
-    return lax.dot_general(a, b, dims, precision=precision, preferred_element_type=F32)
+def dot(a, b, dims=NN):
+    return lax.dot_general(a, b, dims, preferred_element_type=F32)
 
 
 def split(x):
@@ -193,15 +192,6 @@
             copy.start()
             r_copies.append(copy)
 
-    for dx in range(1, xs):
-        for h in range(2):
-            across[dx, h].wait_recv()
-            over[dx, h] = remote(
-                far.at[2 * dx, piece[h]], far.at[2 * dx + 1, piece[h]],
-                fp_ss.at[2 * dx + 1, h], fp_rs.at[2 * dx + 1, h], plane_id(0, 1),
-            )
-            over[dx, h].start()
-
     places = []
     for k in range(blocks):
         owner = bt[k] // tiles
@@ -240,7 +230,7 @@
         blocks_here = far.at[slot] if slot else fp
 
         def add(start):
-            def pair(i, carry):
+            def pair(i):
                 rows = []
                 for b in range(2):
                     parts = []
@@ -253,9 +243,9 @@
                 for b in range(2):
                     part = total[b * releases : (b + 1) * releases]
                     mat[2 * i + b] = part if fresh else mat[2 * i + b] + part
-                return carry
-
-            lax.fori_loop(0, share // 2, pair, 0)
+
+            for i in range(share // 2):
+                pair(i)
 
         if blocks == group:
             add(0)
@@ -265,8 +255,19 @@
             fresh = False
             lax.fori_loop(0, blocks // group, lambda g, c: (add(g * group), c)[1], 0)
 
+    def pass_on(h):
+        for dx in range(1, xs):
+            across[dx, h].wait_recv()
+            over[dx, h] = remote(
+                far.at[2 * dx, piece[h]], far.at[2 * dx + 1, piece[h]],
+                fp_ss.at[2 * dx + 1, h], fp_rs.at[2 * dx + 1, h], plane_id(0, 1),
+            )
+            over[dx, h].start()
+
+    pass_on(0)
     wrows[...] = w_out[here].astype(F32)
     gram(0, True)
+    pass_on(1)
 
     for copy in r_copies:
         copy.wait_recv()
@@ -285,9 +286,8 @@
     loads[5].wait()
     loads[6].wait()
     first = (mx * 2 + mc) * share
-    want = lax.broadcasted_iota(jnp.int32, (share, bins), 0) + first
-    chosen = (lax.broadcasted_iota(jnp.int32, (share, bins), 1) == want).astype(F32)
-    lr_t, mean_t, pw_t = (dot(chosen, ref[...], NN, HIGHEST) for ref in (lr, mean, pw))
+    mine = pl.ds(pl.multiple_of(first, share), share)
+    lr_t, mean_t, pw_t = (ref[mine, :] for ref in (lr, mean, pw))
     inverse_slope = 1.0 + jnp.exp(-lr_t)
     extra = pw_t * inverse_slope * inverse_slope
 
@@ -377,6 +377,20 @@
             moved = jnp.where(inside, 0.0, old) - dot(left, right, TN)
             mat[b] = moved
             mat[b, base : base + PANEL, :] = new
+
+
+def hand_out_kernel(pieces, updated, residual, updated_out, residual_out, sems):
+    size = residual.shape[0] // pieces
+    copies = [pltpu.make_async_copy(updated, updated_out, sems.at[pieces])]
+    for n in range(pieces):
+        part = pl.ds(n * size, size)
+        copies.append(
+            pltpu.make_async_copy(residual.at[part], residual_out.at[part], sems.at[n])
+        )
+    for copy in copies:
+        copy.start()
+    for copy in copies:
+        copy.wait()
 
 
 def body(
@@ -432,6 +446,19 @@
         footprint, block_tile, log_release.T, prior_mean.T, prior_weight.T, observed,
         noise_weight, pixel_mask,
     )
+    pieces = math.gcd(tiles, 4)
+    updated, residual = pl.pallas_call(
+        functools.partial(hand_out_kernel, pieces),
+        out_shape=(
+            jax.ShapeDtypeStruct(updated.shape, F32),
+            jax.ShapeDtypeStruct(residual.shape, F32),
+        ),
+        in_specs=[hbm, hbm],
+        out_specs=(hbm, hbm),
+        scratch_shapes=[dma((pieces + 1,))],
+        compiler_params=pltpu.CompilerParams(vmem_limit_bytes=60 * 2**20),
+        name="hand_out",
+    )(updated, residual)
     return (updated.T, residual)
 
 

time: 33.8 us -> 35.2 us (1.041)
  Pallas kernels: 30.1 us -> 34.4 us
  local copies, waits for them, and re-layouts: 2.82 us -> 0 us
    pallas_call x0 -> x1, Pallas kernels: none -> 5.24 us  [body(): pl.pallas_call(functools.partial(hand_out_kernel, pieces), out_shape=(jax...]
    unnamed x4 -> x0, local copies, waits for them, and re-layouts: 2.82 us -> none
    pallas_call x1, Pallas kernels: 30.1 us -> 29.2 us  [body(): pl.pallas_call(functools.partial(step_kernel, owners, xs, share, cap), ou...]
where the time goes in v2:
time: 35.2 us; the launch traced here: 35.1 us
  Pallas kernels  34.4 us (98%)
  between operations  0.64 us (2%)
    pallas_call x1, Pallas kernels, body(): pl.pallas_call(functools.partial(step_kernel, owners, xs, share, cap), ou...  29.2 us
    pallas_call x1, Pallas kernels, body(): pl.pallas_call(functools.partial(hand_out_kernel, pieces), out_shape=(jax...  5.24 us

profile of v2, /device:TPU:0, one launch (start us, length us, event | category | flops | bytes accessed | tf_op | source)
XLA Modules:
  0.0 35.1 jit_solution(16602647312750737909)
XLA Ops:
  0.6 29.2 %newton_step.1 = (f32[8,32,128]{2,1,0:T(8,128)}, f32[8,128]{1,0:T(8,128)}) custom-call(bf16[6,128,128]{2,1,0:T(8,128)(2,1)} %fp_hbm.1, s32[6]{0:T(128)} %bt.1, f32[32,128]{1,0:T(8,128)} %bitcast.4, f32[32,128]{1,0:T(8,128)} %bitcast.5, f32[32,128]{1,0:T(8,128)} %bitcast.6, f32[8,32,128]{2,1,0:T(8,128)} %obs_hbm.1, f32[8,32,128]{2,1,0:T(8,128)} %noise_hbm.1, ...), custom_call_target="tpu_custom_call" | custom-call | tf_op jit(solution)/shard_map/newton_step/pallas_call | solution.py:411
  29.8 5.2 %hand_out.1 = (f32[8,128]{1,0:T(8,128)}, f32[8,32,128]{2,1,0:T(8,128)}) custom-call(f32[8,128]{1,0:T(8,128)} %get-tuple-element.6.updated, f32[8,32,128]{2,1,0:T(8,128)} %get-tuple-element.7.residual), custom_call_target="tpu_custom_call" | custom-call | tf_op jit(solution)/shard_map/hand_out/pallas_call | solution.py:450

commit v3 on v2

--- a/solution.py
+++ b/solution.py
@@ -379,17 +379,25 @@
             mat[b, base : base + PANEL, :] = new
 
 
-def hand_out_kernel(pieces, updated, residual, updated_out, residual_out, sems):
+def hand_out_kernel(
+    pieces, updated, residual, updated_out, residual_out, small, large, in_s, out_s
+):
     size = residual.shape[0] // pieces
-    copies = [pltpu.make_async_copy(updated, updated_out, sems.at[pieces])]
-    for n in range(pieces):
-        part = pl.ds(n * size, size)
-        copies.append(
-            pltpu.make_async_copy(residual.at[part], residual_out.at[part], sems.at[n])
-        )
-    for copy in copies:
+    parts = [pl.ds(n * size, size) for n in range(pieces)]
+    views = [(updated, small, updated_out)]
+    views += [(residual.at[p], large.at[p], residual_out.at[p]) for p in parts]
+    arriving = [
+        pltpu.make_async_copy(src, mid, in_s.at[n]) for n, (src, mid, _) in enumerate(views)
+    ]
+    leaving = [
+        pltpu.make_async_copy(mid, dst, out_s.at[n]) for n, (_, mid, dst) in enumerate(views)
+    ]
+    for copy in arriving:
         copy.start()
-    for copy in copies:
+    for first, second in zip(arriving, leaving):
+        first.wait()
+        second.start()
+    for copy in leaving:
         copy.wait()
 
 
@@ -446,7 +454,7 @@
         footprint, block_tile, log_release.T, prior_mean.T, prior_weight.T, observed,
         noise_weight, pixel_mask,
     )
-    pieces = math.gcd(tiles, 4)
+    pieces = math.gcd(tiles, 2)
     updated, residual = pl.pallas_call(
         functools.partial(hand_out_kernel, pieces),
         out_shape=(
@@ -455,7 +463,10 @@
         ),
         in_specs=[hbm, hbm],
         out_specs=(hbm, hbm),
-        scratch_shapes=[dma((pieces + 1,))],
+        scratch_shapes=[
+            pltpu.VMEM(updated.shape, F32), pltpu.VMEM(residual.shape, F32),
+            dma((pieces + 1,)), dma((pieces + 1,)),
+        ],
         compiler_params=pltpu.CompilerParams(vmem_limit_bytes=60 * 2**20),
         name="hand_out",
     )(updated, residual)

time: 35.2 us -> 31.6 us (0.90)
  Pallas kernels: 34.4 us -> 30.7 us
    pallas_call x1, Pallas kernels: 5.24 us -> 1.56 us  [body(): pl.pallas_call(functools.partial(hand_out_kernel, pieces), out_shape=(jax...]
where the time goes in v3:
time: 31.6 us; the launch traced here: 31.4 us
  Pallas kernels  30.7 us (97%)
  between operations  0.64 us (2%)
    pallas_call x1, Pallas kernels, body(): pl.pallas_call(functools.partial(step_kernel, owners, xs, share, cap), ou...  29.2 us
    pallas_call x1, Pallas kernels, body(): pl.pallas_call(functools.partial(hand_out_kernel, pieces), out_shape=(jax...  1.56 us

profile of v3, /device:TPU:0, one launch (start us, length us, event | category | flops | bytes accessed | tf_op | source)
XLA Modules:
  0.0 31.4 jit_solution(2302801932784582716)
XLA Ops:
  0.6 29.2 %newton_step.1 = (f32[8,32,128]{2,1,0:T(8,128)}, f32[8,128]{1,0:T(8,128)}) custom-call(bf16[6,128,128]{2,1,0:T(8,128)(2,1)} %fp_hbm.1, s32[6]{0:T(128)} %bt.1, f32[32,128]{1,0:T(8,128)} %bitcast.4, f32[32,128]{1,0:T(8,128)} %bitcast.5, f32[32,128]{1,0:T(8,128)} %bitcast.6, f32[8,32,128]{2,1,0:T(8,128)} %obs_hbm.1, f32[8,32,128]{2,1,0:T(8,128)} %noise_hbm.1, ...), custom_call_target="tpu_custom_call" | custom-call | tf_op jit(solution)/shard_map/newton_step/pallas_call | solution.py:419
  29.8 1.6 %hand_out.1 = (f32[8,128]{1,0:T(8,128)}, f32[8,32,128]{2,1,0:T(8,128)}) custom-call(f32[8,128]{1,0:T(8,128)} %get-tuple-element.6.updated, f32[8,32,128]{2,1,0:T(8,128)} %get-tuple-element.7.residual), custom_call_target="tpu_custom_call" | custom-call | tf_op jit(solution)/shard_map/hand_out/pallas_call | solution.py:458
